TPU v7x, 32 devices: a whole 2x2x4 slice. The times are simulated.
32 devices in a mesh: row: 16 (over z, y, x), head: 2 (over core).
Axes of the slice: x: 2, y: 2, z: 4, core: 2. Of those that a mesh axis runs over, the one named last changes fastest.
Arguments:
- query_single: bfloat16 [16, 384], P('row'), may hold values from -6 to 6
- key_single: bfloat16 [1024, 384], P('row'), may hold values from -6 to 6
- pair: bfloat16 [16, 1024, 128], P('row'), may hold values from -6 to 32
- query_frames: float32 [12, 16], P(None, 'row'), may hold values from -2.5 to 2.5, as said below
- key_frames: float32 [12, 1024], P(None, 'row'), may hold values from -2.5 to 2.5, as said below
- w_query: bfloat16 [384, 96], P(None, 'head'), may hold values from -0.3125 to 0.3125
- w_key: bfloat16 [384, 96], P(None, 'head'), may hold values from -0.3125 to 0.3125
- w_value: bfloat16 [384, 96], P(None, 'head'), may hold values from -0.3125 to 0.3125
- w_query_points: bfloat16 [384, 72], P(None, 'head'), may hold values from -0.3125 to 0.3125
- w_key_points: bfloat16 [384, 72], P(None, 'head'), may hold values from -0.3125 to 0.3125
- w_value_points: bfloat16 [384, 144], P(None, 'head'), may hold values from -0.3125 to 0.3125
- head_weight: float32 [6], P('head'), may hold values from -2.5 to 0.5
- bias_weight: bfloat16 [6, 128], P('head'), as said below
- w_out: bfloat16 [1056, 384], P('head'), may hold values from -0.1875 to 0.1875
- d_out: bfloat16 [16, 384], P('row'), may hold values from -24 to 24
Outputs:
- output: bfloat16 [16, 384], P('row')
- grad_query: float32 [16, 384], P('row')
- grad_keys: float32 [1024, 384], P('row')
Inputs may be any that keep to these rules, and one draw needn't show every extreme that they name: `bias_weight`: entries within -2.5 and 2.5 over the square root of 128. `query_frames`: rows 0 to 8 of each column form a rotation matrix. `key_frames`: rows 0 to 8 of each column form a rotation matrix.
All inputs are finite; a program needn't handle non-finite values.
Results may differ from a plain program's by a relative error of at most 0.012.
The roundings to bfloat16 on the way count: a program that leaves them out, or rounds other values in their place, can miss the bound.
Values may be sent and summed in bfloat16 or wider, within the bound.
No kernel may reach another device: no remote copies, remote signals or barrier semaphores. Data moves between devices by JAX's collectives and lax.ppermute only.
A program may use at most 64 MiB of HBM per device.

v0:
```python
import functools
import math

import jax
import jax.numpy as jnp
from jax import lax
from jax.experimental import pallas as pl
from jax.experimental.pallas import tpu as pltpu
from jax.sharding import PartitionSpec as P

C = 16
PQ = 4
PV = 8
LANES = 128
SUBLANES = 8
ROWS16 = 16
LOGIT_SCALE = math.sqrt(1.0 / 3.0)
POINT_SCALE = math.sqrt(2.0 / (9.0 * PQ))
F32 = jnp.float32
B16 = jnp.bfloat16


class Layout:
    def __init__(self, heads):
        self.heads = heads
        self.base = heads * C
        self.kp = heads * PQ
        self.vp = heads * PV
        self.square = self.base + 3 * self.kp
        assert self.square + self.kp <= LANES and self.base + 3 * self.vp <= LANES
        assert 2 * heads + 2 <= SUBLANES and PQ == 4


def nn(a, b, precision=None):
    return lax.dot_general(a, b, (((1,), (0,)), ((), ())), precision=precision, preferred_element_type=F32)


def nt(a, b):
    return lax.dot_general(a, b, (((1,), (1,)), ((), ())), preferred_element_type=F32)


def iota(shape, dim):
    return lax.broadcasted_iota(jnp.int32, shape, dim)


def pick(condition):
    return jnp.where(condition, 1.0, 0.0).astype(B16)


def to_lane(rows, offset):
    j, i = iota((LANES, rows), 0), iota((LANES, rows), 1)
    return pick(j == i + offset)


def to_components(rows, offset, points, seg):
    j, i = iota((LANES, rows), 0), iota((LANES, rows), 1)
    found = j < 0
    for c in range(3):
        m = j - (c * seg + offset)
        found = found | ((m >= 0) & (m < points) & (i == 3 * m + c))
    return pick(found)


def unpack(tile, seg):
    return tile, pltpu.roll(tile, LANES - seg, 1), pltpu.roll(tile, LANES - 2 * seg, 1)


def pack(parts, seg, base):
    lane = iota(parts[0].shape, 1)
    keep = (lane >= base) & (lane < base + seg)
    x, y, z = (jnp.where(keep, v, 0.0) for v in parts)
    return x + pltpu.roll(y, seg, 1) + pltpu.roll(z, 2 * seg, 1)


def head_of(shape, lay):
    lane = iota(shape, 1)
    zero = jnp.full(shape, -1, jnp.int32)
    one = jnp.full(shape, -1, jnp.int32)
    for h in range(lay.heads):
        same = (lane >= h * C) & (lane < (h + 1) * C)
        zero, one = jnp.where(same, h, zero), jnp.where(same, h, one)
        for c in range(3):
            k = lay.base + c * lay.kp + h * PQ
            v = lay.base + c * lay.vp + h * PV
            zero = jnp.where((lane >= k) & (lane < k + PQ), h, zero)
            one = jnp.where((lane >= v) & (lane < v + PV), h, one)
    return zero, one


def turned_by(frames, vectors):
    x, y, z = vectors
    return [frames[3 * c] * x + frames[3 * c + 1] * y + frames[3 * c + 2] * z for c in range(3)]


def turned_back(frames, vectors):
    x, y, z = vectors
    return [frames[d] * x + frames[3 + d] * y + frames[6 + d] * z for d in range(3)]


def key_kernel(lay, head_weight, key_single, frames, w_key, w_value, w_kp, w_vp, packed, parcel, turned, gains):
    kp, vp, base = lay.kp, lay.vp, lay.base
    zero = nn(to_lane(base, 0), w_key[...]) + nn(to_components(3 * kp, base, kp, kp), w_kp[...])
    one = nn(to_lane(base, 0), w_value[...]) + nn(to_components(3 * vp, base, vp, vp), w_vp[...])
    w_all = jnp.concatenate([zero, one], axis=0).astype(B16)
    rows = nt(key_single[...], w_all)
    turn = jnp.transpose(frames[...])
    columns = [turn[:, i : i + 1] for i in range(12)]
    tiles = []
    lane = iota((rows.shape[0], LANES), 1)
    for tile, seg in ((rows[:, :LANES], kp), (rows[:, LANES:], vp)):
        moved = turned_by(columns, unpack(tile, seg))
        moved = [(v + columns[9 + c]).astype(B16).astype(F32) for c, v in enumerate(moved)]
        if seg == kp:
            square = moved[0] * moved[0] + moved[1] * moved[1] + moved[2] * moved[2]
        tiles.append(jnp.where(lane < base, tile, 0.0) + pack(moved, seg, base))
    square = square + pltpu.roll(square, LANES - 1, 1)
    square = square + pltpu.roll(square, LANES - 2, 1)
    square = pltpu.roll(square, lay.square - base, 1)
    square = jnp.where((lane >= lay.square) & (lane < lay.square + kp) & ((lane - lay.square) % PQ == 0), square, 0.0)
    first = square.astype(B16).astype(F32)
    second = (square - first).astype(B16).astype(F32)
    third = square - first - second
    tile0 = tiles[0] + first + pltpu.roll(second, 1, 1) + pltpu.roll(third, 2, 1)
    tile0 = tile0.astype(B16)
    packed[:, :LANES] = tile0
    packed[:, LANES:] = tiles[1].astype(B16)
    block = tile0.shape[0]
    parcel[: 2 * LANES, :] = w_all
    parcel[2 * LANES :, :] = jnp.zeros((block + ROWS16, parcel.shape[1]), B16)
    parcel[2 * LANES : 2 * LANES + block, :LANES] = tile0
    turned[:, : turn.shape[1]] = turn
    gain = gain_rows(head_weight, lay)
    gains[...] = gain
    gain = jnp.broadcast_to(gain_lanes(gain, lay), (ROWS16, LANES))
    first = gain.astype(B16).astype(F32)
    second = (gain - first).astype(B16).astype(F32)
    row = iota(gain.shape, 0)
    pieces = jnp.where(row == 0, first, jnp.where(row == 1, second, jnp.where(row == 2, gain - first - second, 0.0)))
    parcel[2 * LANES + block :, :LANES] = pieces.astype(B16)


def gain_rows(head_weight, lay):
    row = iota((SUBLANES, LANES), 0)
    raw = jnp.zeros((SUBLANES, LANES), F32)
    for h in range(lay.heads):
        raw = jnp.where(row == h, jnp.broadcast_to(head_weight[:, h : h + 1], raw.shape), raw)
    gain = (jnp.maximum(raw, 0.0) + jnp.log1p(jnp.exp(-jnp.abs(raw)))) * POINT_SCALE
    return jnp.where(row < lay.heads, gain, 0.0)


def gain_lanes(gain, lay):
    zero, _ = head_of(gain.shape, lay)
    return jnp.sum(jnp.where(zero == iota(gain.shape, 0), gain, 0.0), axis=0, keepdims=True)


def early_kernel(
    lay, block, order, frames, query_single, w_query, w_qp, bias_weight, w_out, d_out, pair, gains,
    left, base, d_base, d_row, w_out_rows, w_query_rows, table, pair_rows, scratch,
):
    me = lax.axis_index("row")
    for place, offset in enumerate(order):
        j = pl.multiple_of((me ^ offset) * block, block)
        pair_rows[place * block : (place + 1) * block, :] = pair[0, pl.ds(j, block), :]
    turn = [jnp.broadcast_to(frames[:, i : i + 1], (1, LANES)) for i in range(12)]
    for i in range(12):
        table[i : i + 1, :] = turn[i]
    heads, start = lay.heads, lay.base
    width = C + 4 * PV + LANES
    near = C + 4 * PV
    shape = (SUBLANES, LANES)
    row, lane = iota(shape, 0), iota(shape, 1)
    zero_head, _ = head_of(shape, lay)
    w_q = nn(to_lane(start, 0), w_query[...]) + nn(to_components(3 * lay.kp, start, lay.kp, lay.kp), w_qp[...])
    w_q = w_q.astype(B16)
    w_query_rows[...] = w_q
    w_o = jnp.zeros((2 * LANES, w_out.shape[1]), F32)
    for h in range(heads):
        i, j = iota((2 * LANES, near), 0), iota((2 * LANES, near), 1)
        m = i - (LANES + h * C)
        found = (m >= 0) & (m < C) & (j == m)
        m = i - (start + h * PV)
        found = found | ((m >= 0) & (m < PV) & (j == C + 3 * PV + m))
        for c in range(3):
            m = i - (LANES + start + c * lay.vp + h * PV)
            found = found | ((m >= 0) & (m < PV) & (j == C + 3 * m + c))
        w_o = w_o + nn(pick(found), w_out[h * width : h * width + near, :])
    w_o = w_o.astype(B16)
    w_out_rows[: 2 * LANES, :] = w_o
    for h in range(heads):
        w_out_rows[(2 + h) * LANES : (3 + h) * LANES, :] = w_out[h * width + near : (h + 1) * width, :]
    single = jnp.broadcast_to(query_single[...], (SUBLANES, query_single.shape[1]))
    rows = nt(single, w_q)
    moved = turned_by(turn, unpack(rows, lay.kp))
    points = pack([(v + turn[9 + c]).astype(B16).astype(F32) for c, v in enumerate(moved)], lay.kp, start)
    query = jnp.where(lane < start, rows, 0.0).astype(B16).astype(F32)
    left[:SUBLANES, :] = jnp.where(zero_head == row, query, 0.0)
    minus = lane < 0
    for h in range(heads):
        at = lay.square + h * PQ
        minus = minus | ((row == h) & (lane >= at) & (lane < at + 3))
    mine = jnp.where(zero_head == row, points, 0.0)
    left[SUBLANES:, :] = jnp.where(minus, -0.5, mine)
    gain = gains[...]
    cotangent = jnp.broadcast_to(d_out[...], (SUBLANES, d_out.shape[1]))
    d_row[...] = nt(cotangent, w_o)
    scratch[...] = jnp.zeros_like(scratch)
    scratch[:heads, :] = bias_weight[...].astype(F32)
    for h in range(heads):
        d_pair = nt(cotangent, w_out[h * width + near : (h + 1) * width, :])
        scratch[SUBLANES + h : SUBLANES + h + 1, :] = d_pair[:1, :]
    both = nt(scratch[...].astype(B16), pair_rows[...])
    square = jnp.sum(mine * mine, axis=1, keepdims=True)
    base[...] = both[:SUBLANES] - 0.5 * gain[:, :1] * square
    d_base[...] = both[SUBLANES:]


def attention_kernel(lay, block, order, *refs):
    *parts, left, base, d_base, d_row, gains, table, message, features, weights, scores = refs
    frames = [table[i : i + 1, :] for i in range(12)]
    me = lax.axis_index("row")
    heads, vp, start = lay.heads, lay.vp, lay.base
    shape = (SUBLANES, LANES)
    row, lane = iota(shape, 0), iota(shape, 1)
    _, one_head = head_of(shape, lay)
    gain = gains[...]
    queries = left[...].astype(B16)
    first = jnp.concatenate([nt(queries, part[:, :LANES]) for part in parts], axis=1)
    logits = LOGIT_SCALE * (first[:SUBLANES] * (1.0 / math.sqrt(C)) + base[...] + gain[:, :1] * first[SUBLANES:])
    weight = jnp.exp(logits - jnp.max(logits, axis=1, keepdims=True))
    attention = weight / jnp.sum(weight, axis=1, keepdims=True)
    attention = jnp.where(iota(attention.shape, 0) < heads, attention, 0.0)
    attention_b = attention.astype(B16)
    sums = spread(attention_b, [part.at[:, LANES:] for part in parts])
    weights[...] = attention_b
    sums = jnp.sum(jnp.where(one_head == row, sums, 0.0), axis=0, keepdims=True)
    sums = jnp.broadcast_to(sums, shape)
    local = turned_back(frames, [v - frames[9 + c] for c, v in enumerate(unpack(sums, vp))])
    lengths = jnp.sqrt(1.0 + (local[0] * local[0] + local[1] * local[1] + local[2] * local[2]))
    d_one = d_row[:, LANES:]
    share = d_row[:, :LANES] / lengths
    d_points = turned_by(frames, [v + share * u for v, u in zip(unpack(d_one, vp), local)])
    d_side = jnp.where(lane < start, d_one, 0.0) + pack(d_points, vp, start)
    right = jnp.where(one_head == row, d_side, 0.0).astype(B16)
    d_attention = jnp.concatenate([nt(right, part[:, LANES:]) for part in parts], axis=1) + d_base[...]
    total = jnp.sum(attention * d_attention, axis=1, keepdims=True)
    score_b = (LOGIT_SCALE * attention * (d_attention - total)).astype(B16)
    query = jnp.sum(jnp.where(lane < lay.square, left[:SUBLANES, :] + left[SUBLANES:, :], 0.0), axis=0, keepdims=True)
    side = jnp.where(row == 2 * heads, jnp.broadcast_to(query, shape), 0.0)
    side = side + jnp.where(row == 2 * heads + 1, d_side, 0.0)
    both = attention_b.astype(F32) + pltpu.roll(score_b.astype(F32), heads, 0)
    for at in range(0, both.shape[1], LANES):
        tile = jnp.where(row < 2 * heads, both[:, at : at + LANES], side).astype(B16)
        for place in range(at // block, (at + LANES) // block):
            for core in range(2):
                message[(me ^ order[place]) * 2 + core, :, :] = tile
    scores[...] = score_b
    features[:, :LANES] = jnp.where((lane >= start) & (lane < start + vp), lengths, 0.0)
    features[:, LANES:] = jnp.where(lane < start, sums, 0.0) + pack(local, vp, start)


def spread(weights, parts):
    total, at = 0.0, 0
    for part in parts:
        total = total + nn(weights[:, at : at + part.shape[0]], part[...])
        at += part.shape[0]
    return total


def rows_kernel(lay, *refs):
    *parts, pair, left, scores, features, weights, w_out_rows, w_query_rows, gains, table, sums = refs
    frames = [table[i : i + 1, :] for i in range(12)]
    shape = (SUBLANES, LANES)
    row, lane = iota(shape, 0), iota(shape, 1)
    zero_head, _ = head_of(shape, lay)
    pair_sum = nn(weights[...], pair[...])
    pairs = [jnp.broadcast_to(pair_sum[h : h + 1, :], shape) for h in range(lay.heads)]
    result = nn(jnp.concatenate([features[...]] + pairs, axis=1).astype(B16), w_out_rows[...])
    score = scores[...].astype(F32)
    d_rows = spread(scores[...], [part.at[:, :LANES] for part in parts])
    score_sum = jnp.sum(score, axis=1, keepdims=True)
    points = left[SUBLANES:, :]
    d_rows = jnp.where(lane < lay.base, d_rows * (1.0 / math.sqrt(C)), gains[...] * (d_rows - score_sum * points))
    d_rows = jnp.broadcast_to(
        jnp.sum(jnp.where(zero_head == row, d_rows, 0.0), axis=0, keepdims=True), shape
    )
    local = pack(turned_back(frames, unpack(d_rows, lay.kp)), lay.kp, lay.base)
    both = (jnp.where(lane < lay.base, d_rows, 0.0) + local).astype(B16)
    sums[...] = jnp.concatenate([result, nn(both, w_query_rows[...])], axis=1)


def owner_kernel(lay, near, arrived, turned, parcel, other, result):
    heads, base = lay.heads, lay.base
    count = arrived.shape[0] // 2
    block = turned.shape[0]
    shape = (SUBLANES, LANES)
    whole = (count, SUBLANES, LANES)
    per = LANES // block
    place = ((iota(whole, 0) ^ lax.axis_index("row")) // near) % per
    row = iota(shape, 0)
    zero_head, one_head = head_of(shape, lay)
    lane = iota(shape, 1)
    keep0 = (zero_head >= 0) & (zero_head + heads == row)
    keep1 = one_head == row
    ones = jnp.broadcast_to(jnp.where(keep0 & (lane >= base), 1.0, 0.0)[None], whole)
    columns = [turned[:, i : i + 1] for i in range(9)]
    lane = iota((block, LANES), 1)
    me = lax.axis_index("head")
    total = None
    for core, held in ((me, parcel), (1 - me, other)):
        took = jnp.concatenate([arrived[pl.ds(q * 2 + core, 1)] for q in range(count)], axis=0).astype(F32)
        mine = took
        for part in range(1, per):
            mine = jnp.where(place == part, pltpu.roll(took, LANES - part * block, 2), mine)
        side0 = jnp.where(keep0[None], jnp.broadcast_to(took[:, 2 * heads : 2 * heads + 1, :], whole), 0.0)
        side1 = jnp.where(keep1[None], jnp.broadcast_to(took[:, 2 * heads + 1 : 2 * heads + 2, :], whole), 0.0)
        right = jnp.concatenate([side0, side1, ones], axis=2).reshape(count * SUBLANES, 3 * LANES).astype(B16)
        moved = jnp.transpose(mine.reshape(count * SUBLANES, LANES)).astype(B16)
        both = nn(moved, right)[:block]
        pieces = held[2 * LANES + block :, :LANES].astype(F32)
        gain = pieces[0:1] + pieces[1:2] + pieces[2:3]
        own = held[2 * LANES : 2 * LANES + block, :LANES].astype(F32)
        tile0, tile1 = both[:, :LANES], both[:, LANES : 2 * LANES]
        points = gain * (tile0 - both[:, 2 * LANES :] * own)
        points = pack(turned_back(columns, unpack(points, lay.kp)), lay.kp, base)
        tile0 = jnp.where(lane < base, tile0 * (1.0 / math.sqrt(C)), points)
        points = pack(turned_back(columns, unpack(tile1, lay.vp)), lay.vp, base)
        tile1 = jnp.where(lane < base, tile1, points)
        rows = jnp.concatenate([tile0, tile1], axis=1).astype(B16)
        part = nn(rows, held[: 2 * LANES, :])
        total = part if total is None else total + part
    result[...] = total


def finish_kernel(own, other, output, grad_query):
    width = output.shape[1]
    total = own[...] + other[...]
    output[...] = total[:1, :width].astype(output.dtype)
    grad_query[...] = total[:1, width:]


VMEM = pl.BlockSpec(memory_space=pltpu.VMEM)
HBM = pl.BlockSpec(memory_space=pltpu.HBM)


def call(body, outs, args, fresh=0, scratch=(), flops=1000000, last=False):
    size = sum(math.prod(v.shape) * v.dtype.itemsize for v in list(args) + list(outs))

    def kernel(*refs):
        if fresh:
            *refs, sems = refs
            held = refs[len(refs) - fresh :]
            copies = [pltpu.make_async_copy(refs[i], held[i], sems.at[i]) for i in range(fresh)]
            for copy in copies:
                copy.start()
            for copy in copies:
                copy.wait()
            refs = list(held) + list(refs[fresh : len(refs) - fresh])
        body(*refs)

    own = [pltpu.VMEM(v.shape, v.dtype) for v in args[:fresh]]
    return pl.pallas_call(
        kernel,
        out_shape=tuple(outs),
        in_specs=[HBM] * fresh + [VMEM] * (len(args) - fresh),
        out_specs=tuple([pl.BlockSpec() if last else VMEM] * len(outs)),
        scratch_shapes=list(scratch) + own + ([pltpu.SemaphoreType.DMA((fresh,))] if fresh else []),
        compiler_params=pltpu.CompilerParams(vmem_limit_bytes=(16 << 20) + 6 * size),
        cost_estimate=pl.CostEstimate(flops=flops, bytes_accessed=size, transcendentals=0),
    )(*[pltpu.with_memory_space_constraint(v, pltpu.HBM) for v in args[:fresh]], *args[fresh:])


def shape_of(*dims, dtype=F32):
    return jax.ShapeDtypeStruct(dims, dtype)


def shards(
    query_single, key_single, pair, query_frames, key_frames, w_query, w_key, w_value, w_query_points, w_key_points,
    w_value_points, head_weight, bias_weight, w_out, d_out,
):
    lay = Layout(head_weight.shape[0])
    count = lax.axis_size("row")
    block, width = key_single.shape
    total = count * block
    near = 1
    while 4 * near * near <= count:
        near *= 2
    assert count & (count - 1) == 0

    def exchange(value, mask):
        return lax.ppermute(value, "row", [(i, i ^ mask) for i in range(count)])

    packed, parcel, turned, gains = call(
        functools.partial(key_kernel, lay),
        [
            shape_of(block, 2 * LANES, dtype=B16), shape_of(2 * LANES + block + ROWS16, width, dtype=B16),
            shape_of(block, LANES), shape_of(SUBLANES, LANES),
        ],
        [
            head_weight.reshape(1, -1), key_single, key_frames, w_key.T, w_value.T, w_key_points.T, w_value_points.T,
        ],
        7,
    )
    offsets = [0] + list(range(count - near, 0, -near))
    line = jnp.concatenate([packed] + [exchange(packed, mask) for mask in offsets[1:]], axis=0)
    planes = [0] + list(range(near - 1, 0, -1))
    parts = [line] + [exchange(line, m) for m in planes[1:]]
    order = [m ^ o for m in planes for o in offsets]

    swap = [(i, (i + 1) % 2) for i in range(2)]
    other = lax.ppermute(parcel, "head", swap)
    left, base, d_base, d_row, w_out_rows, w_query_rows, table, pair_rows = call(
        functools.partial(early_kernel, lay, block, order),
        [
            shape_of(ROWS16, LANES), shape_of(SUBLANES, total), shape_of(SUBLANES, total),
            shape_of(SUBLANES, 2 * LANES), shape_of((2 + lay.heads) * LANES, width, dtype=B16),
            shape_of(LANES, width, dtype=B16), shape_of(ROWS16, LANES),
            shape_of(total, LANES, dtype=B16),
        ],
        [
            query_frames.T, query_single, w_query.T, w_query_points.T, bias_weight, w_out, d_out, pair, gains,
        ],
        8,
        [pltpu.VMEM((ROWS16, LANES), F32)],
    )
    message, features, weight_rows, scores = call(
        functools.partial(attention_kernel, lay, block, order),
        [
            shape_of(2 * count, SUBLANES, LANES, dtype=B16), shape_of(SUBLANES, 2 * LANES),
            shape_of(SUBLANES, total, dtype=B16), shape_of(SUBLANES, total, dtype=B16),
        ],
        parts + [left, base, d_base, d_row, gains, table],
    )
    arrived = lax.all_to_all(message, ("row", "head"), 0, 0, tiled=True)
    (sums,) = call(
        functools.partial(rows_kernel, lay),
        [shape_of(SUBLANES, 2 * width)],
        parts + [pair_rows, left, scores, features, weight_rows, w_out_rows, w_query_rows, gains, table],
    )
    output, grad_query = call(
        finish_kernel,
        [shape_of(1, width, dtype=B16), shape_of(1, width)],
        [sums, lax.ppermute(sums, "head", swap)],
        last=True,
    )
    (grad_keys,) = call(
        functools.partial(owner_kernel, lay, near),
        [shape_of(block, width)],
        [arrived, turned, parcel, other],
        last=True,
    )
    return (output, grad_query, grad_keys)


def solution(mesh):
    return jax.shard_map(
        shards,
        mesh=mesh,
        in_specs=(
            P("row", None),
            P("row", None),
            P("row", None, None),
            P(None, "row"),
            P(None, "row"),
            P(None, "head"),
            P(None, "head"),
            P(None, "head"),
            P(None, "head"),
            P(None, "head"),
            P(None, "head"),
            P("head"),
            P("head", None),
            P("head", None),
            P("row", None),
        ),
        out_specs=(P("row", None), P("row", None), P("row", None)),
        check_vma=False,
    )
```

profile of v0, /device:TPU:0, one launch (start us, length us, event | category | flops | bytes accessed | tf_op | source)
XLA Modules:
  0.0 33.9 jit_solution(9340039070635472990)
XLA Ops:
  0.6 1.8 %shard_map.166 = (bf16[64,256]{1,0:T(8,128)(2,1)S(1)}, bf16[336,384]{1,0:T(8,128)(2,1)S(1)}, f32[64,128]{1,0:T(8,128)S(1)}, f32[8,128]{1,0:T(8,128)S(1)}) custom-call(f32[1,3]{1,0:T(1,128)} %bitcast.14, bf16[64,384]{1,0:T(8,128)(2,1)} %refs_1_.2, f32[12,64]{1,0:T(8,128)} %refs_2_.1, bf16[48,384]{1,0:T(8,128)(2,1)} %bitcast.10, bf16[48,384]{1,0:T(8,128)(2,1)} %bitcast.11, ...), custom_call_target="tpu_custom_call" | custom-call | flops 1000000 | bytes 536588 | tf_op jit(solution)/shard_map/pallas_call | solution.py:361
  2.4 5.1 %collective-permute-start = (bf16[64,256]{1,0:T(8,128)(2,1)S(1)}, bf16[64,256]{1,0:T(8,128)(2,1)S(1)}, u32[]{:S(2)}, u32[]{:S(2)}) collective-permute-start(bf16[64,256]{1,0:T(8,128)(2,1)S(1)} %get-tuple-element.21), channel_id=1, source_target_pairs={{0,24},{2,26},{4,28},{6,30},{8,16},{10,18},{12,20},{14,22},{16,8},... | collective-permute-start | bytes 98312 | tf_op jit(solution)/shard_map/ppermute | solution.py:390
  7.6 0.0 collective-permute-start.1
  7.6 0.6 %collective-permute-start.2 = (bf16[64,256]{1,0:T(8,128)(2,1)S(1)}, bf16[64,256]{1,0:T(8,128)(2,1)S(1)}, u32[]{:S(2)}, u32[]{:S(2)}) collective-permute-start(bf16[64,256]{1,0:T(8,128)(2,1)S(1)} %get-tuple-element.21), channel_id=1, source_target_pairs={{0,8},{2,10},{4,12},{6,14},{8,0},{10,2},{12,4},{14,6},{16,24},{18,... | collective-permute-start | bytes 98312 | tf_op jit(solution)/shard_map/ppermute | solution.py:390
  8.2 1.2 %collective-permute-done = bf16[64,256]{1,0:T(8,128)(2,1)S(1)} collective-permute-done((bf16[64,256]{1,0:T(8,128)(2,1)S(1)}, bf16[64,256]{1,0:T(8,128)(2,1)S(1)}, u32[]{:S(2)}, u32[]{:S(2)}) %collective-permute-start) | collective-permute-done | bytes 32800 | tf_op jit(solution)/shard_map/ppermute | solution.py:390
  9.5 2.9 %collective-permute-done.1 = bf16[64,256]{1,0:T(8,128)(2,1)S(1)} collective-permute-done((bf16[64,256]{1,0:T(8,128)(2,1)S(1)}, bf16[64,256]{1,0:T(8,128)(2,1)S(1)}, u32[]{:S(2)}, u32[]{:S(2)}) %collective-permute-start.1) | collective-permute-done | bytes 32800 | tf_op jit(solution)/shard_map/ppermute | solution.py:390
  12.4 0.0 collective-permute-done.2
  12.4 2.5 %collective-permute-start.3 = (bf16[256,256]{1,0:T(8,128)(2,1)S(1)}, bf16[256,256]{1,0:T(8,128)(2,1)S(1)}, u32[]{:S(2)}, u32[]{:S(2)}) collective-permute-start(bf16[256,256]{1,0:T(8,128)(2,1)S(1)} %constant_dynamic-update-slice_fusion.refs_0_), channel_id=1, source_target_pairs={{0,6},{2,4},{4,2},{6,0},{8,14},{10,12},{12,10},{14,8},{16,22},{18,... | collective-permute-start | bytes 393224 | tf_op jit(solution)/shard_map/ppermute | solution.py:390
  14.9 0.5 %collective-permute-start.4 = (bf16[256,256]{1,0:T(8,128)(2,1)S(1)}, bf16[256,256]{1,0:T(8,128)(2,1)S(1)}, u32[]{:S(2)}, u32[]{:S(2)}) collective-permute-start(bf16[256,256]{1,0:T(8,128)(2,1)S(1)} %constant_dynamic-update-slice_fusion.refs_0_), channel_id=1, source_target_pairs={{0,4},{2,6},{4,0},{6,2},{8,12},{10,14},{12,8},{14,10},{16,20},{18,... | collective-permute-start | bytes 393224 | tf_op jit(solution)/shard_map/ppermute | solution.py:390
  15.4 0.5 %collective-permute-start.5 = (bf16[256,256]{1,0:T(8,128)(2,1)S(1)}, bf16[256,256]{1,0:T(8,128)(2,1)S(1)}, u32[]{:S(2)}, u32[]{:S(2)}) collective-permute-start(bf16[256,256]{1,0:T(8,128)(2,1)S(1)} %constant_dynamic-update-slice_fusion.refs_0_), channel_id=1, source_target_pairs={{0,2},{2,0},{4,6},{6,4},{8,10},{10,8},{12,14},{14,12},{16,18},{18,... | collective-permute-start | bytes 393224 | tf_op jit(solution)/shard_map/ppermute | solution.py:390
  15.9 0.0 collective-permute-start.7
  15.9 2.0 %shard_map.167 = (f32[16,128]{1,0:T(8,128)S(1)}, f32[8,1024]{1,0:T(8,128)S(1)}, f32[8,1024]{1,0:T(8,128)S(1)}, f32[8,256]{1,0:T(8,128)S(1)}, bf16[640,384]{1,0:T...) custom-call(f32[1,12]{1,0:T(1,128)} %bitcast.15, ...), custom_call_target="tpu_custom_call" | custom-call | flops 1000000 | bytes 1680688 | tf_op jit(solution)/shard_map/pallas_call | solution.py:361
  18.0 1.7 %collective-permute-done.3.refs_1_ = bf16[256,256]{1,0:T(8,128)(2,1)S(1)} collective-permute-done((bf16[256,256]{1,0:T(8,128)(2,1)S(1)}, bf16[256,256]{1,0:T(8,128)(2,1)S(1)}, u32[]{:S(2)}, u32[]{:S(2)}) %collective-permute-start.3) | collective-permute-done | bytes 131104 | tf_op jit(solution)/shard_map/ppermute | solution.py:390
  19.7 0.8 %collective-permute-done.4.refs_2_ = bf16[256,256]{1,0:T(8,128)(2,1)S(1)} collective-permute-done((bf16[256,256]{1,0:T(8,128)(2,1)S(1)}, bf16[256,256]{1,0:T(8,128)(2,1)S(1)}, u32[]{:S(2)}, u32[]{:S(2)}) %collective-permute-start.4) | collective-permute-done | bytes 131104 | tf_op jit(solution)/shard_map/ppermute | solution.py:390
  20.5 0.0 collective-permute-done.5.refs_3_
  20.5 1.6 %shard_map.168 = (bf16[32,8,128]{2,1,0:T(8,128)(2,1)}, f32[8,256]{1,0:T(8,128)S(1)}, bf16[8,1024]{1,0:T(8,128)(2,1)S(1)}, bf16[8,1024]{1,0:T(8,128)(2,1)S(1)}) custom-call(bf16[256,256]{1,0:T(8,128)(2,1)S(1)} %constant_dynamic-update-slice_fusion.refs_0_, bf16[256,256]{1,0:T(8,128)(2,1)S(1)} %collective-permute-done.3.refs_1_, ...), custom_call_target="tpu_custom_call" | custom-call | flops 1000000 | bytes 724992 | tf_op jit(solution)/shard_map/pallas_call | solution.py:361
  22.0 3.1 %all-to-all-start = ((bf16[32,8,128]{2,1,0:T(8,128)(2,1)}), bf16[32,8,128]{2,1,0:T(8,128)(2,1)S(1)}, u32[]{:S(2)}, u32[]{:S(2)}) async-start(bf16[32,8,128]{2,1,0:T(8,128)(2,1)} %get-tuple-element.36), calls=%async_computation | async-start | bytes 131072 | tf_op jit(solution)/shard_map/all_to_all | solution.py:433
  25.2 0.6 %shard_map.169.refs_0_ = f32[8,768]{1,0:T(8,128)S(1)} custom-call(bf16[256,256]{1,0:T(8,128)(2,1)S(1)} %constant_dynamic-update-slice_fusion.refs_0_, bf16[256,256]{1,0:T(8,128)(2,1)S(1)} %collective-permute-done.3.refs_1_, bf16[256,256]{1,0:T(8,128)(2,1)S(1)} %collective-permute-done.4.refs_2_, bf16[256,256]{1,0:T(8,128)(2,1)S(1)} %collective-permute-done.5.refs_3_, ...), custom_call_target="tpu_custom_call" | custom-call | flops 1000000 | bytes 1462272 | tf_op jit(solution)/shard_map/pallas_call | solution.py:361
  25.8 0.3 collective-permute-start.6
  26.1 0.9 %collective-permute-done.6.refs_1_ = f32[8,768]{1,0:T(8,128)S(1)} collective-permute-done((f32[8,768]{1,0:T(8,128)S(1)}, f32[8,768]{1,0:T(8,128)S(1)}, u32[]{:S(2)}, u32[]{:S(2)}) %collective-permute-start.6) | collective-permute-done | bytes 24608 | tf_op jit(solution)/shard_map/ppermute | solution.py:442
  27.0 0.6 %shard_map.170 = (bf16[1,384]{1,0:T(2,128)(2,1)}, f32[1,384]{1,0:T(1,128)}) custom-call(f32[8,768]{1,0:T(8,128)S(1)} %shard_map.169.refs_0_, f32[8,768]{1,0:T(8,128)S(1)} %collective-permute-done.6.refs_1_), custom_call_target="tpu_custom_call" | custom-call | flops 1000000 | bytes 51456 | tf_op jit(solution)/shard_map/pallas_call | solution.py:361
  27.6 0.0 collective-permute-done.7.refs_3_
  27.6 5.0 %all-to-all-done.refs_0_ = bf16[32,8,128]{2,1,0:T(8,128)(2,1)S(1)} async-done(((bf16[32,8,128]{2,1,0:T(8,128)(2,1)}), bf16[32,8,128]{2,1,0:T(8,128)(2,1)S(1)}, u32[]{:S(2)}, u32[]{:S(2)}) %all-to-all-start) | async-done | bytes 65568 | tf_op jit(solution)/shard_map/all_to_all | solution.py:433
  32.6 1.3 %shard_map.171 = f32[64,384]{1,0:T(8,128)} custom-call(bf16[32,8,128]{2,1,0:T(8,128)(2,1)S(1)} %all-to-all-done.refs_0_, f32[64,128]{1,0:T(8,128)S(1)} %get-tuple-element.37.refs_1_, bf16[336,384]{1,0:T(8,128)(2,1)S(1)} %get-tuple-element.38.refs_2_, bf16[336,384]{1,0:T(8,128)(2,1)S(1)} %collective-permute-done.7.refs_3_), custom_call_target="tpu_custom_call" | custom-call | flops 1000000 | bytes 712704 | tf_op jit(solution)/shard_map/pallas_call | solution.py:361
  (4 shorter events, 0.0 us)
Async XLA Ops:
  2.4 7.0 %collective-permute-start = (bf16[64,256]{1,0:T(8,128)(2,1)S(1)}, bf16[64,256]{1,0:T(8,128)(2,1)S(1)}, u32[]{:S(2)}, u32[]{:S(2)}) collective-permute-start(bf16[64,256]{1,0:T(8,128)(2,1)S(1)} %get-tuple-element.21), channel_id=1, source_target_pairs={{0,24},{2,26},{4,28},{6,30},{8,16},{10,18},{12,20},{14,22},{16,8},... | collective-permute-start | bytes 98312 | tf_op jit(solution)/shard_map/ppermute | solution.py:390
  7.6 4.8 %collective-permute-start.1 = (bf16[64,256]{1,0:T(8,128)(2,1)S(1)}, bf16[64,256]{1,0:T(8,128)(2,1)S(1)}, u32[]{:S(2)}, u32[]{:S(2)}) collective-permute-start(bf16[64,256]{1,0:T(8,128)(2,1)S(1)} %get-tuple-element.21), channel_id=1, source_target_pairs={{0,16},{2,18},{4,20},{6,22},{8,24},{10,26},{12,28},{14,30},{16,0},... | collective-permute-start | bytes 98312 | tf_op jit(solution)/shard_map/ppermute | solution.py:390
  7.6 4.8 %collective-permute-start.2 = (bf16[64,256]{1,0:T(8,128)(2,1)S(1)}, bf16[64,256]{1,0:T(8,128)(2,1)S(1)}, u32[]{:S(2)}, u32[]{:S(2)}) collective-permute-start(bf16[64,256]{1,0:T(8,128)(2,1)S(1)} %get-tuple-element.21), channel_id=1, source_target_pairs={{0,8},{2,10},{4,12},{6,14},{8,0},{10,2},{12,4},{14,6},{16,24},{18,... | collective-permute-start | bytes 98312 | tf_op jit(solution)/shard_map/ppermute | solution.py:390
  12.4 7.3 %collective-permute-start.3 = (bf16[256,256]{1,0:T(8,128)(2,1)S(1)}, bf16[256,256]{1,0:T(8,128)(2,1)S(1)}, u32[]{:S(2)}, u32[]{:S(2)}) collective-permute-start(bf16[256,256]{1,0:T(8,128)(2,1)S(1)} %constant_dynamic-update-slice_fusion.refs_0_), channel_id=1, source_target_pairs={{0,6},{2,4},{4,2},{6,0},{8,14},{10,12},{12,10},{14,8},{16,22},{18,... | collective-permute-start | bytes 393224 | tf_op jit(solution)/shard_map/ppermute | solution.py:390
  14.9 5.6 %collective-permute-start.4 = (bf16[256,256]{1,0:T(8,128)(2,1)S(1)}, bf16[256,256]{1,0:T(8,128)(2,1)S(1)}, u32[]{:S(2)}, u32[]{:S(2)}) collective-permute-start(bf16[256,256]{1,0:T(8,128)(2,1)S(1)} %constant_dynamic-update-slice_fusion.refs_0_), channel_id=1, source_target_pairs={{0,4},{2,6},{4,0},{6,2},{8,12},{10,14},{12,8},{14,10},{16,20},{18,... | collective-permute-start | bytes 393224 | tf_op jit(solution)/shard_map/ppermute | solution.py:390
  15.4 5.1 %collective-permute-start.5 = (bf16[256,256]{1,0:T(8,128)(2,1)S(1)}, bf16[256,256]{1,0:T(8,128)(2,1)S(1)}, u32[]{:S(2)}, u32[]{:S(2)}) collective-permute-start(bf16[256,256]{1,0:T(8,128)(2,1)S(1)} %constant_dynamic-update-slice_fusion.refs_0_), channel_id=1, source_target_pairs={{0,2},{2,0},{4,6},{6,4},{8,10},{10,8},{12,14},{14,12},{16,18},{18,... | collective-permute-start | bytes 393224 | tf_op jit(solution)/shard_map/ppermute | solution.py:390
  15.9 11.6 %collective-permute-start.7 = (bf16[336,384]{1,0:T(8,128)(2,1)S(1)}, bf16[336,384]{1,0:T(8,128)(2,1)S(1)}, u32[]{:S(2)}, u32[]{:S(2)}) collective-permute-start(bf16[336,384]{1,0:T(8,128)(2,1)S(1)} %get-tuple-element.38.refs_2_), channel_id=1, source_target_pairs={{0,1},{1,0},{2,3},{3,2},{4,5},{5,4},{6,7},{7,6},{8,9},{9,8},{10,11... | collective-permute-start | bytes 774152 | tf_op jit(solution)/shard_map/ppermute | solution.py:410
  22.0 10.6 %all-to-all-start = ((bf16[32,8,128]{2,1,0:T(8,128)(2,1)}), bf16[32,8,128]{2,1,0:T(8,128)(2,1)S(1)}, u32[]{:S(2)}, u32[]{:S(2)}) async-start(bf16[32,8,128]{2,1,0:T(8,128)(2,1)} %get-tuple-element.36), calls=%async_computation | async-start | bytes 131072 | tf_op jit(solution)/shard_map/all_to_all | solution.py:433
  25.8 1.2 %collective-permute-start.6 = (f32[8,768]{1,0:T(8,128)S(1)}, f32[8,768]{1,0:T(8,128)S(1)}, u32[]{:S(2)}, u32[]{:S(2)}) collective-permute-start(f32[8,768]{1,0:T(8,128)S(1)} %shard_map.169.refs_0_), channel_id=1, source_target_pairs={{0,1},{1,0},{2,3},{3,2},{4,5},{5,4},{6,7},{7,6},{8,9},{9,8},{10,11... | collective-permute-start | bytes 73736 | tf_op jit(solution)/shard_map/ppermute | solution.py:442
where the time goes:
time: 34.2 us; the launch traced here: 33.9 us
  starting transfers between devices  12.7 us (37%)
  waiting for transfers between devices  12.7 us (37%)
  Pallas kernels  7.86 us (23%)
  between operations  0.67 us (2%)
    ppermute x6, starting transfers between devices, exchange(): return lax.ppermute(value, 'row', [(i, i ^ mask) for i in range(count)])  9.31 us
    pallas_call x6, Pallas kernels, call(): pl.pallas_call(kernel, out_shape=tuple(outs), in_specs=[HBM] * fresh + [V...  7.86 us
    ppermute x6, waiting for transfers between devices, exchange(): return lax.ppermute(value, 'row', [(i, i ^ mask) for i in range(count)])  6.68 us
    all_to_all x1, waiting for transfers between devices, shards(): arrived = lax.all_to_all(message, ('row', 'head'), 0, 0, tiled=True)  5.02 us
    all_to_all x1, starting transfers between devices, shards(): arrived = lax.all_to_all(message, ('row', 'head'), 0, 0, tiled=True)  3.14 us
    ppermute x1, waiting for transfers between devices, shards(): lax.ppermute(sums, 'head', swap)  0.94 us
  transfers between devices with their start and end apart: 9, of which 6 were waited for; matrix products, arithmetic and copies ran while one was open for 0% of the time, Pallas kernels for 14%

commit v1 on v0

--- a/solution.py
+++ b/solution.py
@@ -97,7 +97,7 @@
     return [frames[d] * x + frames[3 + d] * y + frames[6 + d] * z for d in range(3)]
 
 
-def key_kernel(lay, head_weight, key_single, frames, w_key, w_value, w_kp, w_vp, packed, parcel, turned, gains):
+def key_kernel(lay, key_single, frames, w_key, w_value, w_kp, w_vp, packed, weights):
     kp, vp, base = lay.kp, lay.vp, lay.base
     zero = nn(to_lane(base, 0), w_key[...]) + nn(to_components(3 * kp, base, kp, kp), w_kp[...])
     one = nn(to_lane(base, 0), w_value[...]) + nn(to_components(3 * vp, base, vp, vp), w_vp[...])
@@ -121,22 +121,9 @@
     second = (square - first).astype(B16).astype(F32)
     third = square - first - second
     tile0 = tiles[0] + first + pltpu.roll(second, 1, 1) + pltpu.roll(third, 2, 1)
-    tile0 = tile0.astype(B16)
-    packed[:, :LANES] = tile0
+    packed[:, :LANES] = tile0.astype(B16)
     packed[:, LANES:] = tiles[1].astype(B16)
-    block = tile0.shape[0]
-    parcel[: 2 * LANES, :] = w_all
-    parcel[2 * LANES :, :] = jnp.zeros((block + ROWS16, parcel.shape[1]), B16)
-    parcel[2 * LANES : 2 * LANES + block, :LANES] = tile0
-    turned[:, : turn.shape[1]] = turn
-    gain = gain_rows(head_weight, lay)
-    gains[...] = gain
-    gain = jnp.broadcast_to(gain_lanes(gain, lay), (ROWS16, LANES))
-    first = gain.astype(B16).astype(F32)
-    second = (gain - first).astype(B16).astype(F32)
-    row = iota(gain.shape, 0)
-    pieces = jnp.where(row == 0, first, jnp.where(row == 1, second, jnp.where(row == 2, gain - first - second, 0.0)))
-    parcel[2 * LANES + block :, :LANES] = pieces.astype(B16)
+    weights[...] = w_all
 
 
 def gain_rows(head_weight, lay):
@@ -154,9 +141,25 @@
 
 
 def early_kernel(
-    lay, block, order, frames, query_single, w_query, w_qp, bias_weight, w_out, d_out, pair, gains,
-    left, base, d_base, d_row, w_out_rows, w_query_rows, table, pair_rows, scratch,
+    lay, block, order, frames, query_single, w_query, w_qp, bias_weight, w_out, d_out, pair, head_weight, key_frames,
+    packed, weights,
+    left, base, d_base, d_row, w_out_rows, w_query_rows, table, pair_rows, gains, parcel, turned, scratch,
 ):
+    parcel[: 2 * LANES, :] = weights[...]
+    parcel[2 * LANES :, :] = jnp.zeros((block + ROWS16, parcel.shape[1]), B16)
+    parcel[2 * LANES : 2 * LANES + block, :LANES] = packed[:, :LANES]
+    gain = gain_rows(head_weight, lay)
+    gains[...] = gain
+    pieces = jnp.broadcast_to(gain_lanes(gain, lay), (ROWS16, LANES))
+    first = pieces.astype(B16).astype(F32)
+    second = (pieces - first).astype(B16).astype(F32)
+    row = iota(pieces.shape, 0)
+    pieces = jnp.where(
+        row == 0, first, jnp.where(row == 1, second, jnp.where(row == 2, pieces - first - second, 0.0))
+    )
+    parcel[2 * LANES + block :, :LANES] = pieces.astype(B16)
+    turn = jnp.transpose(key_frames[...])
+    turned[:, : turn.shape[1]] = turn
     me = lax.axis_index("row")
     for place, offset in enumerate(order):
         j = pl.multiple_of((me ^ offset) * block, block)
@@ -200,7 +203,6 @@
         minus = minus | ((row == h) & (lane >= at) & (lane < at + 3))
     mine = jnp.where(zero_head == row, points, 0.0)
     left[SUBLANES:, :] = jnp.where(minus, -0.5, mine)
-    gain = gains[...]
     cotangent = jnp.broadcast_to(d_out[...], (SUBLANES, d_out.shape[1]))
     d_row[...] = nt(cotangent, w_o)
     scratch[...] = jnp.zeros_like(scratch)
@@ -288,14 +290,17 @@
     sums[...] = jnp.concatenate([result, nn(both, w_query_rows[...])], axis=1)
 
 
-def owner_kernel(lay, near, arrived, turned, parcel, other, result):
+def owner_kernel(lay, near, offsets, arrived, turned, parcel, other, result):
     heads, base = lay.heads, lay.base
     count = arrived.shape[0] // 2
     block = turned.shape[0]
     shape = (SUBLANES, LANES)
     whole = (count, SUBLANES, LANES)
     per = LANES // block
-    place = ((iota(whole, 0) ^ lax.axis_index("row")) // near) % per
+    apart = (iota(whole, 0) ^ lax.axis_index("row")) // near
+    place = jnp.zeros(whole, jnp.int32)
+    for i, offset in enumerate(offsets):
+        place = jnp.where(apart == offset // near, i % per, place)
     row = iota(shape, 0)
     zero_head, one_head = head_of(shape, lay)
     lane = iota(shape, 1)
@@ -389,39 +394,40 @@
     def exchange(value, mask):
         return lax.ppermute(value, "row", [(i, i ^ mask) for i in range(count)])
 
-    packed, parcel, turned, gains = call(
+    packed, weights = call(
         functools.partial(key_kernel, lay),
         [
-            shape_of(block, 2 * LANES, dtype=B16), shape_of(2 * LANES + block + ROWS16, width, dtype=B16),
-            shape_of(block, LANES), shape_of(SUBLANES, LANES),
+            shape_of(block, 2 * LANES, dtype=B16), shape_of(2 * LANES, width, dtype=B16),
         ],
         [
-            head_weight.reshape(1, -1), key_single, key_frames, w_key.T, w_value.T, w_key_points.T, w_value_points.T,
+            key_single, key_frames, w_key.T, w_value.T, w_key_points.T, w_value_points.T,
         ],
-        7,
-    )
-    offsets = [0] + list(range(count - near, 0, -near))
+        6,
+    )
+    offsets = [0] + [o for o in range(near, count, near) if o != count // 2] + [count // 2]
     line = jnp.concatenate([packed] + [exchange(packed, mask) for mask in offsets[1:]], axis=0)
-    planes = [0] + list(range(near - 1, 0, -1))
+    planes = list(range(near))
     parts = [line] + [exchange(line, m) for m in planes[1:]]
     order = [m ^ o for m in planes for o in offsets]
 
-    swap = [(i, (i + 1) % 2) for i in range(2)]
-    other = lax.ppermute(parcel, "head", swap)
-    left, base, d_base, d_row, w_out_rows, w_query_rows, table, pair_rows = call(
+    left, base, d_base, d_row, w_out_rows, w_query_rows, table, pair_rows, gains, parcel, turned = call(
         functools.partial(early_kernel, lay, block, order),
         [
             shape_of(ROWS16, LANES), shape_of(SUBLANES, total), shape_of(SUBLANES, total),
             shape_of(SUBLANES, 2 * LANES), shape_of((2 + lay.heads) * LANES, width, dtype=B16),
             shape_of(LANES, width, dtype=B16), shape_of(ROWS16, LANES),
-            shape_of(total, LANES, dtype=B16),
+            shape_of(total, LANES, dtype=B16), shape_of(SUBLANES, LANES),
+            shape_of(2 * LANES + block + ROWS16, width, dtype=B16), shape_of(block, LANES),
         ],
         [
-            query_frames.T, query_single, w_query.T, w_query_points.T, bias_weight, w_out, d_out, pair, gains,
+            query_frames.T, query_single, w_query.T, w_query_points.T, bias_weight, w_out, d_out, pair,
+            head_weight.reshape(1, -1), key_frames, packed, weights,
         ],
-        8,
+        10,
         [pltpu.VMEM((ROWS16, LANES), F32)],
     )
+    swap = [(i, (i + 1) % 2) for i in range(2)]
+    other = lax.ppermute(parcel, "head", swap)
     message, features, weight_rows, scores = call(
         functools.partial(attention_kernel, lay, block, order),
         [
@@ -443,7 +449,7 @@
         last=True,
     )
     (grad_keys,) = call(
-        functools.partial(owner_kernel, lay, near),
+        functools.partial(owner_kernel, lay, near, offsets),
         [shape_of(block, width)],
         [arrived, turned, parcel, other],
         last=True,

time: 34.2 us -> 34.4 us (level)
  starting transfers between devices: 12.7 us -> 13.1 us
    all_to_all x1, starting transfers between devices: 3.14 us -> 3.57 us  [shards(): arrived = lax.all_to_all(message, ('row', 'head'), 0, 0, tiled=True)]
where the time goes in v1:
time: 34.4 us; the launch traced here: 34.2 us
  starting transfers between devices  13.1 us (38%)
  waiting for transfers between devices  12.5 us (36%)
  Pallas kernels  7.89 us (23%)
  between operations  0.68 us (2%)
    ppermute x6, starting transfers between devices, exchange(): return lax.ppermute(value, 'row', [(i, i ^ mask) for i in range(count)])  9.23 us
    pallas_call x6, Pallas kernels, call(): pl.pallas_call(kernel, out_shape=tuple(outs), in_specs=[HBM] * fresh + [V...  7.89 us
    ppermute x6, waiting for transfers between devices, exchange(): return lax.ppermute(value, 'row', [(i, i ^ mask) for i in range(count)])  6.53 us
    all_to_all x1, waiting for transfers between devices, shards(): arrived = lax.all_to_all(message, ('row', 'head'), 0, 0, tiled=True)  5.02 us
    all_to_all x1, starting transfers between devices, shards(): arrived = lax.all_to_all(message, ('row', 'head'), 0, 0, tiled=True)  3.57 us
    ppermute x1, waiting for transfers between devices, shards(): lax.ppermute(sums, 'head', swap)  0.94 us
  transfers between devices with their start and end apart: 9, of which 6 were waited for; matrix products, arithmetic and copies ran while one was open for 0% of the time, Pallas kernels for 14%

profile of v1, /device:TPU:0, one launch (start us, length us, event | category | flops | bytes accessed | tf_op | source)
XLA Modules:
  0.0 34.2 jit_solution(15490939235211122630)
XLA Ops:
  0.6 1.8 %shard_map.166 = (bf16[64,256]{1,0:T(8,128)(2,1)S(1)}, bf16[256,384]{1,0:T(8,128)(2,1)S(1)}) custom-call(bf16[64,384]{1,0:T(8,128)(2,1)} %refs_0_.1, f32[12,64]{1,0:T(8,128)} %refs_9_.1, bf16[48,384]{1,0:T(8,128)(2,1)} %bitcast.10, bf16[48,384]{1,0:T(8,128)(2,1)} %bitcast.11, bf16[36,384]{1,0:T(8,128)(2,1)} %bitcast.12, bf16[72,384]{1,0:T(8,128)(2,1)} %bitcast.8), custom_call_target="tpu_custom_call" | custom-call | flops 1000000 | bytes 438272 | tf_op jit(solution)/shard_map/pallas_call | solution.py:366
  2.4 4.1 %collective-permute-start.2 = (bf16[64,256]{1,0:T(8,128)(2,1)S(1)}, bf16[64,256]{1,0:T(8,128)(2,1)S(1)}, u32[]{:S(2)}, u32[]{:S(2)}) collective-permute-start(bf16[64,256]{1,0:T(8,128)(2,1)S(1)} %get-tuple-element.22.refs_10_), channel_id=1, source_target_pairs={{0,16},{2,18},{4,20},{6,22},{8,24},{10,26},{12,28},{14,30},{16,0},... | collective-permute-start | bytes 98312 | tf_op jit(solution)/shard_map/ppermute | solution.py:395
  6.5 1.3 %collective-permute-start.1 = (bf16[64,256]{1,0:T(8,128)(2,1)S(1)}, bf16[64,256]{1,0:T(8,128)(2,1)S(1)}, u32[]{:S(2)}, u32[]{:S(2)}) collective-permute-start(bf16[64,256]{1,0:T(8,128)(2,1)S(1)} %get-tuple-element.22.refs_10_), channel_id=1, source_target_pairs={{0,24},{2,26},{4,28},{6,30},{8,16},{10,18},{12,20},{14,22},{16,8},... | collective-permute-start | bytes 98312 | tf_op jit(solution)/shard_map/ppermute | solution.py:395
  7.9 0.2 collective-permute-start
  8.1 3.7 %collective-permute-done = bf16[64,256]{1,0:T(8,128)(2,1)S(1)} collective-permute-done((bf16[64,256]{1,0:T(8,128)(2,1)S(1)}, bf16[64,256]{1,0:T(8,128)(2,1)S(1)}, u32[]{:S(2)}, u32[]{:S(2)}) %collective-permute-start) | collective-permute-done | bytes 32800 | tf_op jit(solution)/shard_map/ppermute | solution.py:395
  11.8 0.4 %collective-permute-done.1 = bf16[64,256]{1,0:T(8,128)(2,1)S(1)} collective-permute-done((bf16[64,256]{1,0:T(8,128)(2,1)S(1)}, bf16[64,256]{1,0:T(8,128)(2,1)S(1)}, u32[]{:S(2)}, u32[]{:S(2)}) %collective-permute-start.1) | collective-permute-done | bytes 32800 | tf_op jit(solution)/shard_map/ppermute | solution.py:395
  12.2 0.0 collective-permute-done.2
  12.2 2.5 %collective-permute-start.5 = (bf16[256,256]{1,0:T(8,128)(2,1)S(1)}, bf16[256,256]{1,0:T(8,128)(2,1)S(1)}, u32[]{:S(2)}, u32[]{:S(2)}) collective-permute-start(bf16[256,256]{1,0:T(8,128)(2,1)S(1)} %constant_dynamic-update-slice_fusion.refs_0_), channel_id=1, source_target_pairs={{0,6},{2,4},{4,2},{6,0},{8,14},{10,12},{12,10},{14,8},{16,22},{18,... | collective-permute-start | bytes 393224 | tf_op jit(solution)/shard_map/ppermute | solution.py:395
  14.8 0.5 %collective-permute-start.4 = (bf16[256,256]{1,0:T(8,128)(2,1)S(1)}, bf16[256,256]{1,0:T(8,128)(2,1)S(1)}, u32[]{:S(2)}, u32[]{:S(2)}) collective-permute-start(bf16[256,256]{1,0:T(8,128)(2,1)S(1)} %constant_dynamic-update-slice_fusion.refs_0_), channel_id=1, source_target_pairs={{0,4},{2,6},{4,0},{6,2},{8,12},{10,14},{12,8},{14,10},{16,20},{18,... | collective-permute-start | bytes 393224 | tf_op jit(solution)/shard_map/ppermute | solution.py:395
  15.3 0.5 %collective-permute-start.3 = (bf16[256,256]{1,0:T(8,128)(2,1)S(1)}, bf16[256,256]{1,0:T(8,128)(2,1)S(1)}, u32[]{:S(2)}, u32[]{:S(2)}) collective-permute-start(bf16[256,256]{1,0:T(8,128)(2,1)S(1)} %constant_dynamic-update-slice_fusion.refs_0_), channel_id=1, source_target_pairs={{0,2},{2,0},{4,6},{6,4},{8,10},{10,8},{12,14},{14,12},{16,18},{18,... | collective-permute-start | bytes 393224 | tf_op jit(solution)/shard_map/ppermute | solution.py:395
  15.8 2.1 %shard_map.167 = (f32[16,128]{1,0:T(8,128)S(1)}, f32[8,1024]{1,0:T(8,128)S(1)}, f32[8,1024]{1,0:T(8,128)S(1)}, f32[8,256]{1,0:T(8,128)S(1)}, bf16[640,384]{1,0:T...) custom-call(f32[1,12]{1,0:T(1,128)} %bitcast.14, ...), custom_call_target="tpu_custom_call" | custom-call | flops 1000000 | bytes 2203964 | tf_op jit(solution)/shard_map/pallas_call | solution.py:366
  17.9 0.1 collective-permute-start.7
  18.0 1.6 %collective-permute-done.5.refs_3_ = bf16[256,256]{1,0:T(8,128)(2,1)S(1)} collective-permute-done((bf16[256,256]{1,0:T(8,128)(2,1)S(1)}, bf16[256,256]{1,0:T(8,128)(2,1)S(1)}, u32[]{:S(2)}, u32[]{:S(2)}) %collective-permute-start.5) | collective-permute-done | bytes 131104 | tf_op jit(solution)/shard_map/ppermute | solution.py:395
  19.6 0.8 %collective-permute-done.4.refs_2_ = bf16[256,256]{1,0:T(8,128)(2,1)S(1)} collective-permute-done((bf16[256,256]{1,0:T(8,128)(2,1)S(1)}, bf16[256,256]{1,0:T(8,128)(2,1)S(1)}, u32[]{:S(2)}, u32[]{:S(2)}) %collective-permute-start.4) | collective-permute-done | bytes 131104 | tf_op jit(solution)/shard_map/ppermute | solution.py:395
  20.4 0.0 collective-permute-done.3.refs_1_
  20.4 1.6 %shard_map.168 = (bf16[32,8,128]{2,1,0:T(8,128)(2,1)}, f32[8,256]{1,0:T(8,128)S(1)}, bf16[8,1024]{1,0:T(8,128)(2,1)S(1)}, bf16[8,1024]{1,0:T(8,128)(2,1)S(1)}) custom-call(bf16[256,256]{1,0:T(8,128)(2,1)S(1)} %constant_dynamic-update-slice_fusion.refs_0_, bf16[256,256]{1,0:T(8,128)(2,1)S(1)} %collective-permute-done.3.refs_1_, ...), custom_call_target="tpu_custom_call" | custom-call | flops 1000000 | bytes 724992 | tf_op jit(solution)/shard_map/pallas_call | solution.py:366
  21.9 3.6 %all-to-all-start = ((bf16[32,8,128]{2,1,0:T(8,128)(2,1)}), bf16[32,8,128]{2,1,0:T(8,128)(2,1)S(1)}, u32[]{:S(2)}, u32[]{:S(2)}) async-start(bf16[32,8,128]{2,1,0:T(8,128)(2,1)} %get-tuple-element.38), calls=%async_computation | async-start | bytes 131072 | tf_op jit(solution)/shard_map/all_to_all | solution.py:439
  25.5 0.6 %shard_map.169.refs_0_ = f32[8,768]{1,0:T(8,128)S(1)} custom-call(bf16[256,256]{1,0:T(8,128)(2,1)S(1)} %constant_dynamic-update-slice_fusion.refs_0_, bf16[256,256]{1,0:T(8,128)(2,1)S(1)} %collective-permute-done.3.refs_1_, bf16[256,256]{1,0:T(8,128)(2,1)S(1)} %collective-permute-done.4.refs_2_, bf16[256,256]{1,0:T(8,128)(2,1)S(1)} %collective-permute-done.5.refs_3_, ...), custom_call_target="tpu_custom_call" | custom-call | flops 1000000 | bytes 1462272 | tf_op jit(solution)/shard_map/pallas_call | solution.py:366
  26.1 0.3 collective-permute-start.6
  26.4 0.9 %collective-permute-done.6.refs_1_ = f32[8,768]{1,0:T(8,128)S(1)} collective-permute-done((f32[8,768]{1,0:T(8,128)S(1)}, f32[8,768]{1,0:T(8,128)S(1)}, u32[]{:S(2)}, u32[]{:S(2)}) %collective-permute-start.6) | collective-permute-done | bytes 24608 | tf_op jit(solution)/shard_map/ppermute | solution.py:448
  27.3 0.6 %shard_map.170 = (bf16[1,384]{1,0:T(2,128)(2,1)}, f32[1,384]{1,0:T(1,128)}) custom-call(f32[8,768]{1,0:T(8,128)S(1)} %shard_map.169.refs_0_, f32[8,768]{1,0:T(8,128)S(1)} %collective-permute-done.6.refs_1_), custom_call_target="tpu_custom_call" | custom-call | flops 1000000 | bytes 51456 | tf_op jit(solution)/shard_map/pallas_call | solution.py:366
  27.9 0.0 collective-permute-done.7.refs_3_
  27.9 5.0 %all-to-all-done.refs_0_ = bf16[32,8,128]{2,1,0:T(8,128)(2,1)S(1)} async-done(((bf16[32,8,128]{2,1,0:T(8,128)(2,1)}), bf16[32,8,128]{2,1,0:T(8,128)(2,1)S(1)}, u32[]{:S(2)}, u32[]{:S(2)}) %all-to-all-start) | async-done | bytes 65568 | tf_op jit(solution)/shard_map/all_to_all | solution.py:439
  32.9 1.3 %shard_map.171 = f32[64,384]{1,0:T(8,128)} custom-call(bf16[32,8,128]{2,1,0:T(8,128)(2,1)S(1)} %all-to-all-done.refs_0_, f32[64,128]{1,0:T(8,128)S(1)} %get-tuple-element.39.refs_1_, bf16[336,384]{1,0:T(8,128)(2,1)S(1)} %get-tuple-element.40.refs_2_, bf16[336,384]{1,0:T(8,128)(2,1)S(1)} %collective-permute-done.7.refs_3_), custom_call_target="tpu_custom_call" | custom-call | flops 1000000 | bytes 712704 | tf_op jit(solution)/shard_map/pallas_call | solution.py:366
  (4 shorter events, 0.0 us)
Async XLA Ops:
  2.4 9.8 %collective-permute-start.2 = (bf16[64,256]{1,0:T(8,128)(2,1)S(1)}, bf16[64,256]{1,0:T(8,128)(2,1)S(1)}, u32[]{:S(2)}, u32[]{:S(2)}) collective-permute-start(bf16[64,256]{1,0:T(8,128)(2,1)S(1)} %get-tuple-element.22.refs_10_), channel_id=1, source_target_pairs={{0,16},{2,18},{4,20},{6,22},{8,24},{10,26},{12,28},{14,30},{16,0},... | collective-permute-start | bytes 98312 | tf_op jit(solution)/shard_map/ppermute | solution.py:395
  6.5 5.7 %collective-permute-start.1 = (bf16[64,256]{1,0:T(8,128)(2,1)S(1)}, bf16[64,256]{1,0:T(8,128)(2,1)S(1)}, u32[]{:S(2)}, u32[]{:S(2)}) collective-permute-start(bf16[64,256]{1,0:T(8,128)(2,1)S(1)} %get-tuple-element.22.refs_10_), channel_id=1, source_target_pairs={{0,24},{2,26},{4,28},{6,30},{8,16},{10,18},{12,20},{14,22},{16,8},... | collective-permute-start | bytes 98312 | tf_op jit(solution)/shard_map/ppermute | solution.py:395
  7.9 3.9 %collective-permute-start = (bf16[64,256]{1,0:T(8,128)(2,1)S(1)}, bf16[64,256]{1,0:T(8,128)(2,1)S(1)}, u32[]{:S(2)}, u32[]{:S(2)}) collective-permute-start(bf16[64,256]{1,0:T(8,128)(2,1)S(1)} %get-tuple-element.22.refs_10_), channel_id=1, source_target_pairs={{0,8},{2,10},{4,12},{6,14},{8,0},{10,2},{12,4},{14,6},{16,24},{18,... | collective-permute-start | bytes 98312 | tf_op jit(solution)/shard_map/ppermute | solution.py:395
  12.2 7.3 %collective-permute-start.5 = (bf16[256,256]{1,0:T(8,128)(2,1)S(1)}, bf16[256,256]{1,0:T(8,128)(2,1)S(1)}, u32[]{:S(2)}, u32[]{:S(2)}) collective-permute-start(bf16[256,256]{1,0:T(8,128)(2,1)S(1)} %constant_dynamic-update-slice_fusion.refs_0_), channel_id=1, source_target_pairs={{0,6},{2,4},{4,2},{6,0},{8,14},{10,12},{12,10},{14,8},{16,22},{18,... | collective-permute-start | bytes 393224 | tf_op jit(solution)/shard_map/ppermute | solution.py:395
  14.8 5.6 %collective-permute-start.4 = (bf16[256,256]{1,0:T(8,128)(2,1)S(1)}, bf16[256,256]{1,0:T(8,128)(2,1)S(1)}, u32[]{:S(2)}, u32[]{:S(2)}) collective-permute-start(bf16[256,256]{1,0:T(8,128)(2,1)S(1)} %constant_dynamic-update-slice_fusion.refs_0_), channel_id=1, source_target_pairs={{0,4},{2,6},{4,0},{6,2},{8,12},{10,14},{12,8},{14,10},{16,20},{18,... | collective-permute-start | bytes 393224 | tf_op jit(solution)/shard_map/ppermute | solution.py:395
  15.3 5.1 %collective-permute-start.3 = (bf16[256,256]{1,0:T(8,128)(2,1)S(1)}, bf16[256,256]{1,0:T(8,128)(2,1)S(1)}, u32[]{:S(2)}, u32[]{:S(2)}) collective-permute-start(bf16[256,256]{1,0:T(8,128)(2,1)S(1)} %constant_dynamic-update-slice_fusion.refs_0_), channel_id=1, source_target_pairs={{0,2},{2,0},{4,6},{6,4},{8,10},{10,8},{12,14},{14,12},{16,18},{18,... | collective-permute-start | bytes 393224 | tf_op jit(solution)/shard_map/ppermute | solution.py:395
  17.9 10.0 %collective-permute-start.7 = (bf16[336,384]{1,0:T(8,128)(2,1)S(1)}, bf16[336,384]{1,0:T(8,128)(2,1)S(1)}, u32[]{:S(2)}, u32[]{:S(2)}) collective-permute-start(bf16[336,384]{1,0:T(8,128)(2,1)S(1)} %get-tuple-element.40.refs_2_), channel_id=1, source_target_pairs={{0,1},{1,0},{2,3},{3,2},{4,5},{5,4},{6,7},{7,6},{8,9},{9,8},{10,11... | collective-permute-start | bytes 774152 | tf_op jit(solution)/shard_map/ppermute | solution.py:430
  21.9 11.0 %all-to-all-start = ((bf16[32,8,128]{2,1,0:T(8,128)(2,1)}), bf16[32,8,128]{2,1,0:T(8,128)(2,1)S(1)}, u32[]{:S(2)}, u32[]{:S(2)}) async-start(bf16[32,8,128]{2,1,0:T(8,128)(2,1)} %get-tuple-element.38), calls=%async_computation | async-start | bytes 131072 | tf_op jit(solution)/shard_map/all_to_all | solution.py:439
  26.1 1.2 %collective-permute-start.6 = (f32[8,768]{1,0:T(8,128)S(1)}, f32[8,768]{1,0:T(8,128)S(1)}, u32[]{:S(2)}, u32[]{:S(2)}) collective-permute-start(f32[8,768]{1,0:T(8,128)S(1)} %shard_map.169.refs_0_), channel_id=1, source_target_pairs={{0,1},{1,0},{2,3},{3,2},{4,5},{5,4},{6,7},{7,6},{8,9},{9,8},{10,11... | collective-permute-start | bytes 73736 | tf_op jit(solution)/shard_map/ppermute | solution.py:448
